TPU v7x, 32 devices: a whole 2x2x4 slice. The times are simulated.
32 devices in a mesh: groups: 2 (over x), seq: 16 (over z, y, core).
Axes of the slice: x: 2, y: 2, z: 4, core: 2. Of those that a mesh axis runs over, the one named last changes fastest.
Arguments:
- queries: bfloat16 [12288, 2048], P(('groups', 'seq')), parts along dimension 0, may hold values from -6 to 6
- keys: bfloat16 [12288, 2048], P(('groups', 'seq')), parts along dimension 0, may hold values from -6 to 6
- values: bfloat16 [12288, 2048], P(('groups', 'seq')), parts along dimension 0, may hold values from -6 to 6
- out_grad: bfloat16 [12288, 2048], P(('groups', 'seq')), parts along dimension 0, may hold values from -6 to 6
Outputs:
- relaid: bfloat16 [16, 12288, 128], P('seq', 'groups'), parts along dimension 1
- query_grad: bfloat16 [12288, 2048], P(('groups', 'seq')), parts along dimension 0
- key_grad: bfloat16 [12288, 2048], P(('groups', 'seq')), parts along dimension 0
- value_grad: bfloat16 [12288, 2048], P(('groups', 'seq')), parts along dimension 0
There are 2 independent parts, one for each index of `groups`. A program takes and returns all parts, laid end to end along the dimension named above; each array names one. Nothing has to cross between parts.
All inputs are finite; a program needn't handle non-finite values.
Results may differ from a plain program's by a relative error of at most 0.0058.
Values may be sent and summed in bfloat16 or wider, within the bound.
A program may use at most 128 MiB of HBM per device.

v0:
```python
import jax
import jax.numpy as jnp
from jax import lax
from jax.sharding import PartitionSpec as P

DH = 128
eps = 1e-06


def blocks_before(columns, earlier):
    count = columns.shape[0]
    row_ids = lax.broadcasted_iota(jnp.int32, (count, count), 0)
    col_ids = lax.broadcasted_iota(jnp.int32, (count, count), 1)
    if earlier:
        select = (col_ids < row_ids).astype(jnp.float32)
    else:
        select = (col_ids > row_ids).astype(jnp.float32)
    summed = jnp.dot(
        select, columns, precision=lax.Precision.HIGHEST, preferred_element_type=jnp.float32
    )
    return summed


def earlier_sum(local):
    flat = local.reshape(1, -1)
    columns = lax.all_to_all(flat, "seq", split_axis=1, concat_axis=0, tiled=True)
    shifted = blocks_before(columns, True)
    merged = lax.all_to_all(
        shifted.astype(jnp.bfloat16), "seq", split_axis=0, concat_axis=1, tiled=True
    ).astype(shifted.dtype)
    return merged.reshape(local.shape)


def later_sum(local):
    flat = local.reshape(1, -1)
    columns = lax.all_to_all(flat, "seq", split_axis=1, concat_axis=0, tiled=True)
    shifted = blocks_before(columns, False)
    merged = lax.all_to_all(
        shifted.astype(jnp.bfloat16), "seq", split_axis=0, concat_axis=1, tiled=True
    ).astype(shifted.dtype)
    return merged.reshape(local.shape)


def body(queries, keys, values, out_grad):
    rows = queries.shape[0]
    width = queries.shape[1]
    heads = width // DH
    f32 = jnp.float32
    q3 = queries.reshape(rows, heads, DH)
    k3 = keys.reshape(rows, heads, DH)
    v3 = values.reshape(rows, heads, DH)
    row_ids = lax.broadcasted_iota(jnp.int32, (rows, rows), 0)
    col_ids = lax.broadcasted_iota(jnp.int32, (rows, rows), 1)
    causal = (row_ids >= col_ids)[None]
    local_state = jnp.einsum("shd,she->hde", k3, v3, preferred_element_type=f32)
    scores = jnp.einsum("thd,shd->hts", q3, k3, preferred_element_type=f32)
    masked = jnp.where(causal, scores, 0.0).astype(jnp.bfloat16)
    intra = jnp.einsum("hts,shd->thd", masked, v3, preferred_element_type=f32)
    prefix_b = earlier_sum(local_state).astype(jnp.bfloat16)
    inter = jnp.einsum("thd,hde->the", q3, prefix_b, preferred_element_type=f32)
    acc = intra + inter
    norm = jnp.sqrt(jnp.mean(acc * acc, axis=-1, keepdims=True) + eps)
    unit = acc / norm
    out_heads = unit.astype(jnp.bfloat16)
    splits = lax.axis_size("seq") // heads
    piece_rows = rows // splits
    outgoing = out_heads.reshape(splits, piece_rows, heads, DH)
    outgoing = jnp.transpose(outgoing, (0, 2, 1, 3)).reshape(splits * heads, piece_rows, DH)
    relaid = lax.all_to_all(outgoing, "seq", split_axis=0, concat_axis=1, tiled=True)
    grad_rows = out_grad.reshape(rows, heads, DH).astype(f32)
    inner = jnp.mean(grad_rows * unit, axis=-1, keepdims=True)
    d_acc = ((grad_rows - unit * inner) / norm).astype(jnp.bfloat16)
    back_state = jnp.einsum("thd,the->hde", q3, d_acc, preferred_element_type=f32)
    later_b = later_sum(back_state).astype(jnp.bfloat16)
    dscore = jnp.einsum("thd,shd->hts", d_acc, v3, preferred_element_type=f32)
    dscore = jnp.where(causal, dscore, 0.0).astype(jnp.bfloat16)
    query_grad = jnp.einsum("hts,shd->thd", dscore, k3, preferred_element_type=f32)
    query_grad = query_grad + jnp.einsum(
        "the,hde->thd", d_acc, prefix_b, preferred_element_type=f32
    )
    key_grad = jnp.einsum("hts,thd->shd", dscore, q3, preferred_element_type=f32)
    key_grad = key_grad + jnp.einsum("she,hde->shd", v3, later_b, preferred_element_type=f32)
    value_grad = jnp.einsum("hts,the->she", masked, d_acc, preferred_element_type=f32)
    value_grad = value_grad + jnp.einsum("shd,hde->she", k3, later_b, preferred_element_type=f32)
    return (
        relaid,
        query_grad.astype(jnp.bfloat16).reshape(rows, width),
        key_grad.astype(jnp.bfloat16).reshape(rows, width),
        value_grad.astype(jnp.bfloat16).reshape(rows, width),
    )


def solution(mesh):
    return jax.shard_map(
        body,
        mesh=mesh,
        in_specs=(
            P(("groups", "seq"), None),
            P(("groups", "seq"), None),
            P(("groups", "seq"), None),
            P(("groups", "seq"), None),
        ),
        out_specs=(
            P("seq", "groups", None),
            P(("groups", "seq"), None),
            P(("groups", "seq"), None),
            P(("groups", "seq"), None),
        ),
        check_vma=False,
    )
```

profile of v0, /device:TPU:0, one launch (start us, length us, event | category | flops | bytes accessed | tf_op | source)
XLA Modules:
  0.0 182.9 jit_solution(17124694191122851817)
XLA Ops:
  0.6 0.0 copy-start
  0.6 3.1 %copy.111 = bf16[48,8,16,128]{3,2,1,0:T(8,128)(2,1)} copy(bf16[48,8,16,128]{3,1,2,0:T(8,128)(2,1)} %bitcast.126) | data formatting | bytes 3145728
  3.7 2.1 %copy.79 = bf16[384,16,128]{0,2,1:T(8,128)(2,1)S(1)} copy(bf16[384,16,128]{2,1,0:T(8,128)(2,1)} %bitcast.125) | data formatting | bytes 3145728 | tf_op jit(solution)/shard_map/reshape | solution.py:50
  5.9 0.0 copy-done
  5.9 0.0 copy-start.4
  5.9 0.6 fusion.8
  6.5 0.6 copy-done.4
  7.0 32.0 %all_to_all.76 = f32[1,16,16384]{2,0,1:T(1,128)S(1)} all-to-all(f32[1,16,16384]{2,0,1:T(1,128)S(1)} %bitcast.135), channel_id=1, replica_groups=mesh['groups'=2,'seq'=16] {'seq'}, dimensions={1} | all-to-all | bytes 2097152 | tf_op jit(solution)/shard_map/all_to_all | solution.py:26
  39.0 1.2 fusion
  40.2 0.5 broadcast.25
  40.8 0.9 reduce.2
  41.7 1.2 reshape.106
  42.9 5.1 %all-to-all-start.1 = ((bf16[16,2,8192]{2,1,0:T(2,128)(2,1)}), bf16[16,2,8192]{2,1,0:T(2,128)(2,1)}, u32[]{:S(2)}, u32[]{:S(2)}) async-start(bf16[16,2,8192]{2,1,0:T(2,128)(2,1)} %reshape.106), calls=%async_computation.1 | async-start | bytes 1048576 | tf_op jit(solution)/shard_map/all_to_all | solution.py:28
  48.0 0.0 copy-start.6
  48.0 3.2 %copy.86 = f32[384,2048]{0,1:T(8,128)} copy(bf16[384,2048]{1,0:T(8,128)(2,1)} %param.7) | data formatting | bytes 4718592 | tf_op jit(solution)/shard_map/convert_element_type | solution.py:70
  51.2 0.0 copy-done.6
  51.2 4.9 %select_convert_fusion.1 = bf16[16,384,384]{2,1,0:T(8,128)(2,1)} fusion(pred[384,384]{1,0:T(8,128)(4,1)S(1)} %iota_compare_fusion, bf16[384,2048]{1,0:T(8,128)(2,1)} %param.5, bf16[384,2048]{1,0:T(8,128)(2,1)S(1)} %copy-done.6), kind=kOutput, calls=%fused_computation.5 | convolution fusion | flops 608698368 | bytes 8011776 | tf_op jit(solution)/shard_map/thd,shd->hts/dot_general | solution.py:56
  56.2 6.3 %all-to-all-done.1 = bf16[16,2,8192]{2,1,0:T(2,128)(2,1)} async-done(((bf16[16,2,8192]{2,1,0:T(2,128)(2,1)}), bf16[16,2,8192]{2,1,0:T(2,128)(2,1)}, u32[]{:S(2)}, u32[]{:S(2)}) %all-to-all-start.1) | async-done | bytes 524320 | tf_op jit(solution)/shard_map/all_to_all | solution.py:28
  62.5 3.5 %reshape.107 = bf16[16,1,16384]{2,1,0:T(2,128)(2,1)} reshape(bf16[16,2,8192]{2,1,0:T(2,128)(2,1)} %all-to-all-done.1) | data formatting | bytes 1048576
  65.9 5.1 %reduce = bf16[16,16384]{1,0:T(8,128)(2,1)} reduce(bf16[16,1,16384]{2,1,0:T(2,128)(2,1)} %reshape.107, bf16[]{:T(256)} %constant.8), dimensions={1}, to_apply=%all_to_all.61.reduce_sub_computation | reduce | bytes 1048578 | tf_op jit(solution)/shard_map/all_to_all | solution.py:28
  71.0 1.1 copy.112
  72.1 0.0 copy-start.10
  72.2 0.0 copy-start.2
  72.2 0.8 fusion.16
  73.0 0.0 copy-done.10
  73.0 1.7 copy-done.2
  74.7 1.6 multiply_reduce_fusion.1
  76.3 0.3 copy-done.1
  76.6 0.6 multiply_reduce_fusion
  77.2 0.0 copy-start.7
  77.2 2.0 %divide_convert_fusion = (bf16[384,16,128]{0,2,1:T(8,128)(2,1)S(1)}, bf16[16,384,128]{1,2,0:T(8,128)(2,1)}) fusion(f32[384,16]{0,1:T(8,128)S(1)} %broadcast_multiply_fusion, f32[384,16]{0,1:T(8,128)S(1)} %add_sqrt_fusion, f32[384,2048]{0,1:T(8,128)S(1)} %copy-done.1, f32[384,16,128]{0,2,1:T(8,128)S(1)} %get-tuple-element.23), kind=kLoop, calls=%fused_computation.12 | loop fusion | flops 4718592 | bytes 9486336 | tf_op jit(solution)/shard_map/convert_element_type | solution.py:72
  79.2 0.0 copy-done.7
  79.2 1.6 fusion.20
  80.8 2.5 %copy.93 = f32[16,128,128]{2,1,0:T(8,128)} copy(f32[16,128,128]{1,2,0:T(8,128)} %fusion.20) | data formatting | bytes 2097152 | tf_op jit(solution)/shard_map/thd,the->hde/dot_general | solution.py:73
  83.3 28.9 %all_to_all.77 = f32[1,16,16384]{2,0,1:T(1,128)S(1)} all-to-all(f32[1,16,16384]{2,0,1:T(1,128)} %bitcast.134), channel_id=1, replica_groups=mesh['groups'=2,'seq'=16] {'seq'}, dimensions={1} | all-to-all | bytes 2097152 | tf_op jit(solution)/shard_map/all_to_all | solution.py:36
  112.2 2.0 %fusion.1 = bf16[16,1,16384]{2,0,1:T(8,128)(2,1)} fusion(f32[1,16,16384]{2,0,1:T(1,128)S(1)} %all_to_all.77), kind=kOutput, calls=%fused_computation.3 | convolution fusion | flops 50594048 | bytes 1572864 | tf_op jit(solution)/shard_map/dot_general | solution.py:18
  114.2 2.6 %reduce.3 = bf16[16,16384]{1,0:T(8,128)(2,1)} reduce(bf16[16,1,16384]{2,0,1:T(8,128)(2,1)} %fusion.1, bf16[]{:T(256)} %broadcast.25), dimensions={1}, to_apply=%copy.95.reduce_sub_computation | reduce | bytes 1048578 | tf_op jit(solution)/shard_map/all_to_all | solution.py:38
  116.9 2.2 %reshape.108 = bf16[16,2,8192]{2,1,0:T(2,128)(2,1)} reshape(bf16[16,16384]{1,0:T(8,128)(2,1)} %reduce.3) | data formatting | bytes 1048576
  119.1 19.6 %all_to_all.78 = bf16[16,2,8192]{2,1,0:T(2,128)(2,1)} all-to-all(bf16[16,2,8192]{2,1,0:T(2,128)(2,1)} %reshape.108), channel_id=1, replica_groups=mesh['groups'=2,'seq'=16] {'seq'}, dimensions={0} | all-to-all | bytes 1048576 | tf_op jit(solution)/shard_map/all_to_all | solution.py:38
  138.7 4.6 %all-to-all-start.2 = ((bf16[16,384,128]{1,2,0:T(8,128)(2,1)}), bf16[16,384,128]{1,2,0:T(8,128)(2,1)}, u32[]{:S(2)}, u32[]{:S(2)}) async-start(bf16[16,384,128]{1,2,0:T(8,128)(2,1)} %get-tuple-element.21), calls=%async_computation.2 | async-start | bytes 3145728 | tf_op jit(solution)/shard_map/all_to_all | solution.py:69
  143.3 1.6 fusion.35
  144.9 0.0 copy-start.5
  144.9 1.7 select_convert_fusion
  146.6 0.0 copy-done.5
  146.6 0.0 copy-start.3
  146.6 2.7 %fusion.3 = bf16[384,16,128]{0,2,1:T(8,128)(2,1)} fusion(f32[16,128,384]{2,1,0:T(8,128)S(1)} %fusion.35, bf16[16,384,384]{2,1,0:T(8,128)(2,1)S(1)} %select_convert_fusion, bf16[384,16,128]{0,2,1:T(8,128)(2,1)S(1)} %copy-done.5), kind=kOutput, calls=%fused_computation.9 | convolution fusion | flops 605552640 | bytes 11010048 | tf_op jit(solution)/shard_map/hts,shd->thd/dot_general | solution.py:77
  149.3 0.0 copy-done.3
  149.3 2.6 %copy.99 = bf16[384,2048]{1,0:T(8,128)(2,1)} copy(bf16[384,2048]{0,1:T(8,128)(2,1)} %bitcast.127) | data formatting | bytes 3145728
  151.9 5.2 %fusion.36 = f32[16,128,384]{2,1,0:T(8,128)} fusion(bf16[384,16,128]{0,2,1:T(8,128)(2,1)S(1)} %get-tuple-element.20, bf16[16,384,384]{2,1,0:T(8,128)(2,1)} %select_convert_fusion.1), kind=kOutput, calls=%fused_computation.52 | convolution fusion | flops 603979776 | bytes 9437184 | tf_op jit(solution)/shard_map/hts,the->she/dot_general | solution.py:83
  157.1 3.5 %reshape.109 = bf16[16,1,16384]{2,1,0:T(2,128)(2,1)} reshape(bf16[16,2,8192]{2,1,0:T(2,128)(2,1)} %all_to_all.78) | data formatting | bytes 1048576
  160.6 5.2 %reduce.1 = bf16[16,16384]{1,0:T(8,128)(2,1)} reduce(bf16[16,1,16384]{2,1,0:T(2,128)(2,1)} %reshape.109, bf16[]{:T(256)} %constant.8), dimensions={1}, to_apply=%all_to_all.69.reduce_sub_computation | reduce | bytes 1048578 | tf_op jit(solution)/shard_map/all_to_all | solution.py:38
  165.8 1.1 copy.113
  166.9 0.0 copy-start.11
  166.9 0.0 copy-done.9
  166.9 4.0 %add_convert_fusion = bf16[16,128,384]{2,1,0:T(8,128)(2,1)} fusion(f32[16,128,384]{2,1,0:T(8,128)} %fusion.36, bf16[16,128,128]{2,1,0:T(8,128)(2,1)S(1)} %bitcast.132, bf16[384,2048]{1,0:T(8,128)(2,1)S(1)} %copy-done.9), kind=kOutput, calls=%fused_computation.11 | convolution fusion | flops 202899456 | bytes 6815744 | tf_op jit(solution)/shard_map/shd,hde->she/dot_general | solution.py:84
  170.9 0.0 copy-done.11
  170.9 2.6 %copy.101 = bf16[384,2048]{1,0:T(8,128)(2,1)} copy(bf16[384,2048]{0,1:T(8,128)(2,1)} %bitcast.129) | data formatting | bytes 3145728
  173.6 0.0 copy-done.12
  173.6 0.8 fusion.5
  174.4 0.6 copy-done.8
  175.0 3.7 %fusion.2 = bf16[384,16,128]{0,2,1:T(8,128)(2,1)S(1)} fusion(f32[16,128,384]{2,1,0:T(8,128)S(1)} %fusion.5, bf16[16,384,384]{2,1,0:T(8,128)(2,1)} %copy-done.3, bf16[384,2048]{1,0:T(8,128)(2,1)S(1)} %copy-done.8), kind=kOutput, calls=%fused_computation.7 | convolution fusion | flops 605552640 | bytes 11010048 | tf_op jit(solution)/shard_map/hts,thd->shd/dot_general | solution.py:81
  178.7 1.6 copy.100
  180.3 0.0 all-to-all-done.2
  180.3 2.6 %copy.85 = bf16[16,384,128]{2,1,0:T(8,128)(2,1)} copy(bf16[16,384,128]{1,2,0:T(8,128)(2,1)} %all-to-all-done.2) | data formatting | bytes 3145728 | tf_op jit(solution)/shard_map/all_to_all | solution.py:69
  (7 shorter events, 0.1 us)
Async XLA Ops:
  0.6 5.2 %copy-start = (bf16[384,2048]{1,0:T(8,128)(2,1)S(1)}, bf16[384,2048]{1,0:T(8,128)(2,1)}, u32[]{:S(2)}) copy-start(bf16[384,2048]{1,0:T(8,128)(2,1)} %param.6) | copy-start | bytes 4718596
  5.9 1.1 copy-start.4
  42.9 19.6 %all-to-all-start.1 = ((bf16[16,2,8192]{2,1,0:T(2,128)(2,1)}), bf16[16,2,8192]{2,1,0:T(2,128)(2,1)}, u32[]{:S(2)}, u32[]{:S(2)}) async-start(bf16[16,2,8192]{2,1,0:T(2,128)(2,1)} %reshape.106), calls=%async_computation.1 | async-start | bytes 1048576 | tf_op jit(solution)/shard_map/all_to_all | solution.py:28
  48.0 3.3 %copy-start.6 = (bf16[384,2048]{1,0:T(8,128)(2,1)S(1)}, bf16[384,2048]{1,0:T(8,128)(2,1)}, u32[]{:S(2)}) copy-start(bf16[384,2048]{1,0:T(8,128)(2,1)} %param.4) | copy-start | bytes 4718596
  72.1 0.8 copy-start.10
  72.2 2.5 %copy-start.2 = (bf16[16,384,384]{2,1,0:T(8,128)(2,1)S(1)}, bf16[16,384,384]{2,1,0:T(8,128)(2,1)}, u32[]{:S(2)}) copy-start(bf16[16,384,384]{2,1,0:T(8,128)(2,1)} %select_convert_fusion.1) | copy-start | bytes 14155780
  74.7 1.9 %copy-start.1 = (f32[384,2048]{0,1:T(8,128)S(1)}, f32[384,2048]{0,1:T(8,128)}, u32[]{:S(2)}) copy-start(f32[384,2048]{0,1:T(8,128)} %copy.86) | copy-start | bytes 9437188
  77.2 2.0 %copy-start.7 = (bf16[384,2048]{1,0:T(8,128)(2,1)S(1)}, bf16[384,2048]{1,0:T(8,128)(2,1)}, u32[]{:S(2)}) copy-start(bf16[384,2048]{1,0:T(8,128)(2,1)} %param.4) | copy-start | bytes 4718596
  138.7 41.7 %all-to-all-start.2 = ((bf16[16,384,128]{1,2,0:T(8,128)(2,1)}), bf16[16,384,128]{1,2,0:T(8,128)(2,1)}, u32[]{:S(2)}, u32[]{:S(2)}) async-start(bf16[16,384,128]{1,2,0:T(8,128)(2,1)} %get-tuple-element.21), calls=%async_computation.2 | async-start | bytes 3145728 | tf_op jit(solution)/shard_map/all_to_all | solution.py:69
  144.9 1.7 copy-start.5
  146.6 2.7 %copy-start.3 = (bf16[16,384,384]{2,1,0:T(8,128)(2,1)}, bf16[16,384,384]{2,1,0:T(8,128)(2,1)S(1)}, u32[]{:S(2)}) copy-start(bf16[16,384,384]{2,1,0:T(8,128)(2,1)S(1)} %select_convert_fusion) | copy-start | bytes 14155780
  160.6 6.3 %copy-start.9 = (bf16[384,2048]{1,0:T(8,128)(2,1)S(1)}, bf16[384,2048]{1,0:T(8,128)(2,1)}, u32[]{:S(2)}) copy-start(bf16[384,2048]{1,0:T(8,128)(2,1)} %param.5) | copy-start | bytes 4718596
  166.9 4.1 %copy-start.11 = (bf16[2,8,128,128]{3,2,1,0:T(8,128)(2,1)}, bf16[2,8,128,128]{3,2,1,0:T(8,128)(2,1)S(1)}, u32[]{:S(2)}) copy-start(bf16[2,8,128,128]{3,2,1,0:T(8,128)(2,1)S(1)} %copy.113) | copy-start | bytes 1572868
  170.9 2.6 %copy-start.12 = (bf16[2,8,128,128]{3,2,1,0:T(8,128)(2,1)S(1)}, bf16[2,8,128,128]{3,2,1,0:T(8,128)(2,1)}, u32[]{:S(2)}) copy-start(bf16[2,8,128,128]{3,2,1,0:T(8,128)(2,1)} %copy-done.11) | copy-start | bytes 1572868
  173.6 1.4 copy-start.8
where the time goes:
time: 184 us; the launch traced here: 183 us
  blocking collectives  80.5 us (44%)
  local copies, waits for them, and re-layouts  36.6 us (20%)
  matrix products  32.4 us (18%)
  other arithmetic  16.5 us (9%)
  starting transfers between devices  9.68 us (5%)
  waiting for transfers between devices  6.29 us (3%)
    all_to_all x1, blocking collectives, earlier_sum(): lax.all_to_all(flat, 'seq', split_axis=1, concat_axis=0, tiled=True)  32 us
    all_to_all x1, blocking collectives, later_sum(): lax.all_to_all(flat, 'seq', split_axis=1, concat_axis=0, tiled=True)  28.9 us
    unnamed x36, local copies, waits for them, and re-layouts  25.7 us
    all_to_all x1, blocking collectives, later_sum(): lax.all_to_all(shifted.astype(jnp.bfloat16), 'seq', split_axis=0, concat_...  19.6 us
    all_to_all x2, other arithmetic, later_sum(): lax.all_to_all(shifted.astype(jnp.bfloat16), 'seq', split_axis=0, concat_...  7.82 us
    all_to_all x1, waiting for transfers between devices, earlier_sum(): lax.all_to_all(shifted.astype(jnp.bfloat16), 'seq', split_axis=0, concat_...  6.29 us
    all_to_all x2, other arithmetic, earlier_sum(): lax.all_to_all(shifted.astype(jnp.bfloat16), 'seq', split_axis=0, concat_...  6.02 us
    dot_general x1, matrix products, body(): jnp.einsum('hts,the->she', masked, d_acc, preferred_element_type=f32)  5.18 us
  transfers between devices with their start and end apart: 2, of which 1 were waited for; matrix products, arithmetic and copies ran while one was open for 24% of the time, Pallas kernels for 0%

commit v1 on v0

--- a/solution.py
+++ b/solution.py
@@ -5,6 +5,28 @@
 
 DH = 128
 eps = 1e-06
+
+
+def cut_along(x, dim, devices):
+    before, after = (x.shape[:dim], x.shape[dim + 1 :])
+    return jnp.moveaxis(x.reshape(*before, devices, -1, *after), dim, 0)
+
+
+def laid_out(tiles, dim):
+    tiles = jnp.moveaxis(tiles, 0, dim)
+    shape = tiles.shape
+    return tiles.reshape(*shape[:dim], shape[dim] * shape[dim + 1], *shape[dim + 2 :])
+
+
+def sent_to_each(x, axis, split_dim, concat_dim):
+    peers, index = (lax.axis_size(axis), lax.axis_index(axis))
+    blocks = cut_along(x, split_dim, peers)
+    finished = [blocks[index]]
+    for step in range(1, peers):
+        sent = blocks[(index + step) % peers]
+        finished.append(lax.ppermute(sent, axis, [(i, (i + step) % peers) for i in range(peers)]))
+    blocks = jnp.stack(finished)[(index - jnp.arange(peers)) % peers]
+    return laid_out(blocks, concat_dim)
 
 
 def blocks_before(columns, earlier):
@@ -33,7 +55,7 @@
 
 def later_sum(local):
     flat = local.reshape(1, -1)
-    columns = lax.all_to_all(flat, "seq", split_axis=1, concat_axis=0, tiled=True)
+    columns = sent_to_each(flat, "seq", 1, 0)
     shifted = blocks_before(columns, False)
     merged = lax.all_to_all(
         shifted.astype(jnp.bfloat16), "seq", split_axis=0, concat_axis=1, tiled=True

time: 184 us -> 192 us (1.043)
  blocking collectives: 80.5 us -> 52.4 us
  starting transfers between devices: 9.68 us -> 27 us
  waiting for transfers between devices: 6.29 us -> 18.1 us
  local copies, waits for them, and re-layouts: 36.6 us -> 44 us
    all_to_all x1 -> x0, blocking collectives: 28.9 us -> none  [later_sum(): lax.all_to_all(flat, 'seq', split_axis=1, concat_axis=0, tiled=True)]
    ppermute x0 -> x15, starting transfers between devices: none -> 17.4 us  [sent_to_each(): lax.ppermute(sent, axis, [(i, (i + step) % peers) for i in range(peers)])]
    ppermute x0 -> x15, waiting for transfers between devices: none -> 12 us  [sent_to_each(): lax.ppermute(sent, axis, [(i, (i + step) % peers) for i in range(peers)])]
    another operation x0 -> x2, local copies, waits for them, and re-layouts: none -> 4.61 us  [the longest x1 3.2 us: sent_to_each(): blocks = jnp.stack(finished)[(index - jnp.arange(peers)) % peers]]
    gather x0 -> x1, local copies, waits for them, and re-layouts: none -> 1.92 us  [sent_to_each(): blocks = jnp.stack(finished)[(index - jnp.arange(peers)) % peers]]
    unnamed x36 -> x56, local copies, waits for them, and re-layouts: 25.7 us -> 25.6 us
  transfers between devices with their start and end apart: 2 -> 17, of which waited for: 1 -> 7; matrix products, arithmetic and copies ran while one was open for 24% -> 24% of each run, Pallas kernels for 0% -> 0%
where the time goes in v1:
time: 192 us; the launch traced here: 190 us
  blocking collectives  52.4 us (27%)
  local copies, waits for them, and re-layouts  44 us (23%)
  matrix products  32.3 us (17%)
  starting transfers between devices  27 us (14%)
  waiting for transfers between devices  18.1 us (9%)
  other arithmetic  15.4 us (8%)
    all_to_all x1, blocking collectives, earlier_sum(): lax.all_to_all(flat, 'seq', split_axis=1, concat_axis=0, tiled=True)  32 us
    unnamed x56, local copies, waits for them, and re-layouts  25.6 us
    all_to_all x1, blocking collectives, later_sum(): lax.all_to_all(shifted.astype(jnp.bfloat16), 'seq', split_axis=0, concat_...  20.4 us
    ppermute x15, starting transfers between devices, sent_to_each(): lax.ppermute(sent, axis, [(i, (i + step) % peers) for i in range(peers)])  17.4 us
    ppermute x15, waiting for transfers between devices, sent_to_each(): lax.ppermute(sent, axis, [(i, (i + step) % peers) for i in range(peers)])  12 us
    all_to_all x2, other arithmetic, later_sum(): lax.all_to_all(shifted.astype(jnp.bfloat16), 'seq', split_axis=0, concat_...  6.19 us
    all_to_all x1, waiting for transfers between devices, earlier_sum(): lax.all_to_all(shifted.astype(jnp.bfloat16), 'seq', split_axis=0, concat_...  6.09 us
    all_to_all x2, other arithmetic, earlier_sum(): lax.all_to_all(shifted.astype(jnp.bfloat16), 'seq', split_axis=0, concat_...  6.08 us
  transfers between devices with their start and end apart: 17, of which 7 were waited for; matrix products, arithmetic and copies ran while one was open for 24% of the time, Pallas kernels for 0%

profile of v1, /device:TPU:0, one launch (start us, length us, event | category | flops | bytes accessed | tf_op | source)
XLA Modules:
  0.0 190.4 jit_solution(13914523631299267499)
XLA Ops:
  0.6 3.1 %copy.108 = bf16[48,8,16,128]{3,2,1,0:T(8,128)(2,1)} copy(bf16[48,8,16,128]{3,1,2,0:T(8,128)(2,1)} %bitcast.172) | data formatting | bytes 3145728
  3.7 2.1 %copy.78 = bf16[384,16,128]{0,2,1:T(8,128)(2,1)S(1)} copy(bf16[384,16,128]{2,1,0:T(8,128)(2,1)} %bitcast.171) | data formatting | bytes 3145728 | tf_op jit(solution)/shard_map/reshape | solution.py:72
  5.9 0.6 fusion.8
  6.5 0.5 copy-done.6
  7.0 32.0 %all_to_all.60 = f32[1,16,16384]{2,0,1:T(1,128)S(1)} all-to-all(f32[1,16,16384]{2,0,1:T(1,128)S(1)} %bitcast.180), channel_id=1, replica_groups=mesh['groups'=2,'seq'=16] {'seq'}, dimensions={1} | all-to-all | bytes 2097152 | tf_op jit(solution)/shard_map/all_to_all | solution.py:48
  39.0 1.2 fusion
  40.2 0.6 broadcast.109
  40.8 1.0 reduce.2
  41.8 1.2 reshape.162
  43.0 5.1 %all-to-all-start.1 = ((bf16[16,2,8192]{2,1,0:T(2,128)(2,1)}), bf16[16,2,8192]{2,1,0:T(2,128)(2,1)}, u32[]{:S(2)}, u32[]{:S(2)}) async-start(bf16[16,2,8192]{2,1,0:T(2,128)(2,1)} %reshape.162), calls=%async_computation.1 | async-start | bytes 1048576 | tf_op jit(solution)/shard_map/all_to_all | solution.py:50
  48.3 3.2 %copy.85 = f32[384,2048]{0,1:T(8,128)} copy(bf16[384,2048]{1,0:T(8,128)(2,1)} %param.7) | data formatting | bytes 4718592 | tf_op jit(solution)/shard_map/convert_element_type | solution.py:92
  51.5 5.0 %select_convert_fusion.1 = bf16[16,384,384]{2,1,0:T(8,128)(2,1)} fusion(pred[384,384]{1,0:T(8,128)(4,1)S(1)} %iota_compare_fusion, bf16[384,2048]{1,0:T(8,128)(2,1)} %param.5, bf16[384,2048]{1,0:T(8,128)(2,1)S(1)} %copy-done.8), kind=kOutput, calls=%fused_computation.6 | convolution fusion | flops 608698368 | bytes 8011776 | tf_op jit(solution)/shard_map/thd,shd->hts/dot_general | solution.py:78
  56.5 6.1 %all-to-all-done.1 = bf16[16,2,8192]{2,1,0:T(2,128)(2,1)} async-done(((bf16[16,2,8192]{2,1,0:T(2,128)(2,1)}), bf16[16,2,8192]{2,1,0:T(2,128)(2,1)}, u32[]{:S(2)}, u32[]{:S(2)}) %all-to-all-start.1) | async-done | bytes 524320 | tf_op jit(solution)/shard_map/all_to_all | solution.py:50
  62.6 3.5 %reshape.163 = bf16[16,1,16384]{2,1,0:T(2,128)(2,1)} reshape(bf16[16,2,8192]{2,1,0:T(2,128)(2,1)} %all-to-all-done.1) | data formatting | bytes 1048576
  66.1 5.1 %reduce = bf16[16,16384]{1,0:T(8,128)(2,1)} reduce(bf16[16,1,16384]{2,1,0:T(2,128)(2,1)} %reshape.163, bf16[]{:T(256)} %constant.121), dimensions={1}, to_apply=%all_to_all.49.reduce_sub_computation | reduce | bytes 1048578 | tf_op jit(solution)/shard_map/all_to_all | solution.py:50
  71.1 1.1 copy.109
  72.3 0.8 fusion.16
  73.1 1.7 copy-done.4
  74.8 1.6 multiply_reduce_fusion.1
  76.7 0.6 multiply_reduce_fusion
  77.3 1.9 divide_convert_fusion
  79.2 1.1 copy-done.2
  80.3 1.6 fusion.20
  81.9 2.6 %copy.92 = f32[16,128,128]{2,1,0:T(8,128)} copy(f32[16,128,128]{1,2,0:T(8,128)} %fusion.20) | data formatting | bytes 2097152 | tf_op jit(solution)/shard_map/thd,the->hde/dot_general | solution.py:95
  84.5 1.4 transpose_reshape_reshape.3
  85.9 0.9 dynamic-slice_bitcast_fusion
  86.9 1.2 collective-permute-start.1
  88.0 2.1 %collective-permute-start.2 = (f32[1,16384]{1,0:T(1,128)S(1)}, f32[1,16384]{1,0:T(1,128)S(1)}, u32[]{:S(2)}, u32[]{:S(2)}) collective-permute-start(f32[1,16384]{1,0:T(1,128)S(1)} %get-tuple-element.34), channel_id=1, source_target_pairs={{0,3},{1,4},{2,5},{3,6},{4,7},{5,8},{6,9},{7,10},{8,11},{9,12},{10... | collective-permute-start | bytes 196616 | tf_op jit(solution)/shard_map/ppermute | solution.py:27
  90.1 0.8 collective-permute-start.3
  91.0 2.4 %collective-permute-done = f32[1,16384]{1,0:T(1,128)S(1)} collective-permute-done((f32[1,16384]{1,0:T(1,128)S(1)}, f32[1,16384]{1,0:T(1,128)S(1)}, u32[]{:S(2)}, u32[]{:S(2)}) %collective-permute-start) | collective-permute-done | bytes 65568 | tf_op jit(solution)/shard_map/ppermute | solution.py:27
  93.9 0.6 collective-permute-done.1
  94.5 1.7 collective-permute-start.6
  96.2 1.8 collective-permute-start.7
  98.0 0.8 collective-permute-start.8
  98.7 6.3 %collective-permute-done.4 = f32[1,16384]{1,0:T(1,128)S(1)} collective-permute-done((f32[1,16384]{1,0:T(1,128)S(1)}, f32[1,16384]{1,0:T(1,128)S(1)}, u32[]{:S(2)}, u32[]{:S(2)}) %collective-permute-start.4) | collective-permute-done | bytes 65568 | tf_op jit(solution)/shard_map/ppermute | solution.py:27
  105.3 1.4 collective-permute-start.10
  106.7 2.9 %collective-permute-start.11 = (f32[1,16384]{1,0:T(1,128)S(1)}, f32[1,16384]{1,0:T(1,128)S(1)}, u32[]{:S(2)}, u32[]{:S(2)}) collective-permute-start(f32[1,16384]{1,0:T(1,128)S(1)} %get-tuple-element.25), channel_id=1, source_target_pairs={{0,12},{1,13},{2,14},{3,15},{4,0},{5,1},{6,2},{7,3},{8,4},{9,5},{1... | collective-permute-start | bytes 196616 | tf_op jit(solution)/shard_map/ppermute | solution.py:27
  109.6 1.5 collective-permute-start.12
  111.1 2.5 %collective-permute-start.13 = (f32[1,16384]{1,0:T(1,128)S(1)}, f32[1,16384]{1,0:T(1,128)S(1)}, u32[]{:S(2)}, u32[]{:S(2)}) collective-permute-start(f32[1,16384]{1,0:T(1,128)S(1)} %get-tuple-element.23), channel_id=1, source_target_pairs={{0,14},{1,15},{2,0},{3,1},{4,2},{5,3},{6,4},{7,5},{8,6},{9,7},{10,... | collective-permute-start | bytes 196616 | tf_op jit(solution)/shard_map/ppermute | solution.py:27
  113.7 0.6 pad_clamp_fusion
  114.4 1.7 collective-permute-done.13
  116.1 0.8 collective-permute-done.14
  116.9 0.6 copy-done.22
  117.5 3.2 %stack.63 = f32[16,1,16384]{2,0,1:T(8,128)S(1)} concatenate(f32[1,1,16384]{2,0,1:T(1,128)S(1)} %get-tuple-element.37, f32[1,1,16384]{2,0,1:T(1,128)S(1)} %bitcast.184, f32[1,1,16384]{2,0,1:T(1,128)S(1)} %bitcast.185, f32[1,1,16384]{2,0,1:T(1,128)S(1)} %bitcast.186, f32[1,1,16384]{2,0,1:T(1,128)S(1)} %bitcast.187, f32[1,1,16384]{2,0,1:T(1,128)S(1)} %bitcast.188, ...), dimensions={0} | concatenate | bytes 2097152 | tf_op jit(solution)/shard_map/stack | solution.py:28
  120.7 1.9 %gather_fusion = f32[16,16384]{1,0:T(8,128)} fusion(f32[16,16384]{1,0:T(8,128)S(1)} %bitcast.170, s32[1024]{0:T(1024)} %pad_clamp_fusion), kind=kCustom, calls=%fused_computation | custom fusion | bytes 2097216 | tf_op jit(solution)/shard_map/gather | solution.py:28
  122.6 1.8 fusion.1
  124.4 1.0 reduce.3
  125.8 20.4 %all_to_all.61 = bf16[16,2,8192]{2,1,0:T(2,128)(2,1)} all-to-all(bf16[16,2,8192]{2,1,0:T(2,128)(2,1)S(1)} %reshape.164), channel_id=1, replica_groups=mesh['groups'=2,'seq'=16] {'seq'}, dimensions={0} | all-to-all | bytes 1048576 | tf_op jit(solution)/shard_map/all_to_all | solution.py:60
  146.2 4.5 %all-to-all-start.2 = ((bf16[16,384,128]{1,2,0:T(8,128)(2,1)}), bf16[16,384,128]{1,2,0:T(8,128)(2,1)}, u32[]{:S(2)}, u32[]{:S(2)}) async-start(bf16[16,384,128]{1,2,0:T(8,128)(2,1)} %get-tuple-element.21), calls=%async_computation.2 | async-start | bytes 3145728 | tf_op jit(solution)/shard_map/all_to_all | solution.py:91
  150.7 1.6 fusion.35
  152.4 1.7 select_convert_fusion
  154.1 2.7 %fusion.3 = bf16[384,16,128]{0,2,1:T(8,128)(2,1)} fusion(f32[16,128,384]{2,1,0:T(8,128)S(1)} %fusion.35, bf16[16,384,384]{2,1,0:T(8,128)(2,1)S(1)} %select_convert_fusion, bf16[384,16,128]{0,2,1:T(8,128)(2,1)S(1)} %copy-done.7), kind=kOutput, calls=%fused_computation.10 | convolution fusion | flops 605552640 | bytes 11010048 | tf_op jit(solution)/shard_map/hts,shd->thd/dot_general | solution.py:99
  156.8 2.6 %copy.97 = bf16[384,2048]{1,0:T(8,128)(2,1)} copy(bf16[384,2048]{0,1:T(8,128)(2,1)} %bitcast.173) | data formatting | bytes 3145728
  159.4 5.2 %fusion.36 = f32[16,128,384]{2,1,0:T(8,128)} fusion(bf16[384,16,128]{0,2,1:T(8,128)(2,1)S(1)} %copy-done.3, bf16[16,384,384]{2,1,0:T(8,128)(2,1)} %select_convert_fusion.1), kind=kOutput, calls=%fused_computation.74 | convolution fusion | flops 603979776 | bytes 9437184 | tf_op jit(solution)/shard_map/hts,the->she/dot_general | solution.py:105
  164.6 3.5 %reshape.165 = bf16[16,1,16384]{2,1,0:T(2,128)(2,1)} reshape(bf16[16,2,8192]{2,1,0:T(2,128)(2,1)} %all_to_all.61) | data formatting | bytes 1048576
  168.0 5.2 %reduce.1 = bf16[16,16384]{1,0:T(8,128)(2,1)} reduce(bf16[16,1,16384]{2,1,0:T(2,128)(2,1)} %reshape.165, bf16[]{:T(256)} %constant.121), dimensions={1}, to_apply=%all_to_all.54.reduce_sub_computation | reduce | bytes 1048578 | tf_op jit(solution)/shard_map/all_to_all | solution.py:60
  173.2 1.1 copy.110
  174.4 4.0 %add_convert_fusion = bf16[16,128,384]{2,1,0:T(8,128)(2,1)} fusion(f32[16,128,384]{2,1,0:T(8,128)} %fusion.36, bf16[16,128,128]{2,1,0:T(8,128)(2,1)S(1)} %bitcast.178, bf16[384,2048]{1,0:T(8,128)(2,1)S(1)} %copy-done.10), kind=kOutput, calls=%fused_computation.12 | convolution fusion | flops 202899456 | bytes 6815744 | tf_op jit(solution)/shard_map/shd,hde->she/dot_general | solution.py:106
  178.4 2.6 %copy.99 = bf16[384,2048]{1,0:T(8,128)(2,1)} copy(bf16[384,2048]{0,1:T(8,128)(2,1)} %bitcast.175) | data formatting | bytes 3145728
  181.1 0.8 fusion.5
  181.8 0.6 copy-done.9
  182.5 3.7 %fusion.2 = bf16[384,16,128]{0,2,1:T(8,128)(2,1)S(1)} fusion(f32[16,128,384]{2,1,0:T(8,128)S(1)} %fusion.5, bf16[16,384,384]{2,1,0:T(8,128)(2,1)} %copy-done.5, bf16[384,2048]{1,0:T(8,128)(2,1)S(1)} %copy-done.9), kind=kOutput, calls=%fused_computation.8 | convolution fusion | flops 605552640 | bytes 11010048 | tf_op jit(solution)/shard_map/hts,thd->shd/dot_general | solution.py:103
  186.2 1.6 copy.98
  187.8 2.6 %copy.84 = bf16[16,384,128]{2,1,0:T(8,128)(2,1)} copy(bf16[16,384,128]{1,2,0:T(8,128)(2,1)} %all-to-all-done.2) | data formatting | bytes 3145728 | tf_op jit(solution)/shard_map/all_to_all | solution.py:91
  (62 shorter events, 1.9 us)
Async XLA Ops:
  0.6 5.2 %copy-start = (bf16[384,2048]{1,0:T(8,128)(2,1)S(1)}, bf16[384,2048]{1,0:T(8,128)(2,1)}, u32[]{:S(2)}) copy-start(bf16[384,2048]{1,0:T(8,128)(2,1)} %param.6) | copy-start | bytes 4718596
  5.9 1.1 copy-start.6
  43.0 19.6 %all-to-all-start.1 = ((bf16[16,2,8192]{2,1,0:T(2,128)(2,1)}), bf16[16,2,8192]{2,1,0:T(2,128)(2,1)}, u32[]{:S(2)}, u32[]{:S(2)}) async-start(bf16[16,2,8192]{2,1,0:T(2,128)(2,1)} %reshape.162), calls=%async_computation.1 | async-start | bytes 1048576 | tf_op jit(solution)/shard_map/all_to_all | solution.py:50
  48.3 3.2 %copy-start.8 = (bf16[384,2048]{1,0:T(8,128)(2,1)S(1)}, bf16[384,2048]{1,0:T(8,128)(2,1)}, u32[]{:S(2)}) copy-start(bf16[384,2048]{1,0:T(8,128)(2,1)} %param.4) | copy-start | bytes 4718596
  72.3 0.9 copy-start.11
  72.3 2.5 %copy-start.4 = (bf16[16,384,384]{2,1,0:T(8,128)(2,1)S(1)}, bf16[16,384,384]{2,1,0:T(8,128)(2,1)}, u32[]{:S(2)}) copy-start(bf16[16,384,384]{2,1,0:T(8,128)(2,1)} %select_convert_fusion.1) | copy-start | bytes 14155780
  74.8 1.9 copy-start.1
  79.2 1.1 copy-start.2
  86.8 6.6 %collective-permute-start = (f32[1,16384]{1,0:T(1,128)S(1)}, f32[1,16384]{1,0:T(1,128)S(1)}, u32[]{:S(2)}, u32[]{:S(2)}) collective-permute-start(f32[1,16384]{1,0:T(1,128)S(1)} %get-tuple-element.36), channel_id=1, source_target_pairs={{0,1},{1,2},{2,3},{3,4},{4,5},{5,6},{6,7},{7,8},{8,9},{9,10},{10,1... | collective-permute-start | bytes 196616 | tf_op jit(solution)/shard_map/ppermute | solution.py:27
  86.9 7.7 %collective-permute-start.1 = (f32[1,16384]{1,0:T(1,128)S(1)}, f32[1,16384]{1,0:T(1,128)S(1)}, u32[]{:S(2)}, u32[]{:S(2)}) collective-permute-start(f32[1,16384]{1,0:T(1,128)S(1)} %get-tuple-element.35), channel_id=1, source_target_pairs={{0,2},{1,3},{2,4},{3,5},{4,6},{5,7},{6,8},{7,9},{8,10},{9,11},{10,... | collective-permute-start | bytes 196616 | tf_op jit(solution)/shard_map/ppermute | solution.py:27
  88.0 8.2 %collective-permute-start.2 = (f32[1,16384]{1,0:T(1,128)S(1)}, f32[1,16384]{1,0:T(1,128)S(1)}, u32[]{:S(2)}, u32[]{:S(2)}) collective-permute-start(f32[1,16384]{1,0:T(1,128)S(1)} %get-tuple-element.34), channel_id=1, source_target_pairs={{0,3},{1,4},{2,5},{3,6},{4,7},{5,8},{6,9},{7,10},{8,11},{9,12},{10... | collective-permute-start | bytes 196616 | tf_op jit(solution)/shard_map/ppermute | solution.py:27
  90.1 7.9 %collective-permute-start.3 = (f32[1,16384]{1,0:T(1,128)S(1)}, f32[1,16384]{1,0:T(1,128)S(1)}, u32[]{:S(2)}, u32[]{:S(2)}) collective-permute-start(f32[1,16384]{1,0:T(1,128)S(1)} %get-tuple-element.33), channel_id=1, source_target_pairs={{0,4},{1,5},{2,6},{3,7},{4,8},{5,9},{6,10},{7,11},{8,12},{9,13},{1... | collective-permute-start | bytes 196616 | tf_op jit(solution)/shard_map/ppermute | solution.py:27
  90.9 14.2 %collective-permute-start.4 = (f32[1,16384]{1,0:T(1,128)S(1)}, f32[1,16384]{1,0:T(1,128)S(1)}, u32[]{:S(2)}, u32[]{:S(2)}) collective-permute-start(f32[1,16384]{1,0:T(1,128)S(1)} %get-tuple-element.32), channel_id=1, source_target_pairs={{0,5},{1,6},{2,7},{3,8},{4,9},{5,10},{6,11},{7,12},{8,13},{9,14},{... | collective-permute-start | bytes 196616 | tf_op jit(solution)/shard_map/ppermute | solution.py:27
  93.3 11.9 %collective-permute-start.5 = (f32[1,16384]{1,0:T(1,128)S(1)}, f32[1,16384]{1,0:T(1,128)S(1)}, u32[]{:S(2)}, u32[]{:S(2)}) collective-permute-start(f32[1,16384]{1,0:T(1,128)S(1)} %get-tuple-element.31), channel_id=1, source_target_pairs={{0,6},{1,7},{2,8},{3,9},{4,10},{5,11},{6,12},{7,13},{8,14},{9,15},... | collective-permute-start | bytes 196616 | tf_op jit(solution)/shard_map/ppermute | solution.py:27
  94.5 12.2 %collective-permute-start.6 = (f32[1,16384]{1,0:T(1,128)S(1)}, f32[1,16384]{1,0:T(1,128)S(1)}, u32[]{:S(2)}, u32[]{:S(2)}) collective-permute-start(f32[1,16384]{1,0:T(1,128)S(1)} %get-tuple-element.30), channel_id=1, source_target_pairs={{0,7},{1,8},{2,9},{3,10},{4,11},{5,12},{6,13},{7,14},{8,15},{9,0},... | collective-permute-start | bytes 196616 | tf_op jit(solution)/shard_map/ppermute | solution.py:27
  96.2 13.4 %collective-permute-start.7 = (f32[1,16384]{1,0:T(1,128)S(1)}, f32[1,16384]{1,0:T(1,128)S(1)}, u32[]{:S(2)}, u32[]{:S(2)}) collective-permute-start(f32[1,16384]{1,0:T(1,128)S(1)} %get-tuple-element.29), channel_id=1, source_target_pairs={{0,8},{1,9},{2,10},{3,11},{4,12},{5,13},{6,14},{7,15},{8,0},{9,1},... | collective-permute-start | bytes 196616 | tf_op jit(solution)/shard_map/ppermute | solution.py:27
  98.0 13.1 %collective-permute-start.8 = (f32[1,16384]{1,0:T(1,128)S(1)}, f32[1,16384]{1,0:T(1,128)S(1)}, u32[]{:S(2)}, u32[]{:S(2)}) collective-permute-start(f32[1,16384]{1,0:T(1,128)S(1)} %get-tuple-element.28), channel_id=1, source_target_pairs={{0,9},{1,10},{2,11},{3,12},{4,13},{5,14},{6,15},{7,0},{8,1},{9,2},... | collective-permute-start | bytes 196616 | tf_op jit(solution)/shard_map/ppermute | solution.py:27
  105.1 8.6 %collective-permute-start.9 = (f32[1,16384]{1,0:T(1,128)S(1)}, f32[1,16384]{1,0:T(1,128)S(1)}, u32[]{:S(2)}, u32[]{:S(2)}) collective-permute-start(f32[1,16384]{1,0:T(1,128)S(1)} %get-tuple-element.27), channel_id=1, source_target_pairs={{0,10},{1,11},{2,12},{3,13},{4,14},{5,15},{6,0},{7,1},{8,2},{9,3},... | collective-permute-start | bytes 196616 | tf_op jit(solution)/shard_map/ppermute | solution.py:27
  105.3 9.1 %collective-permute-start.10 = (f32[1,16384]{1,0:T(1,128)S(1)}, f32[1,16384]{1,0:T(1,128)S(1)}, u32[]{:S(2)}, u32[]{:S(2)}) collective-permute-start(f32[1,16384]{1,0:T(1,128)S(1)} %get-tuple-element.26), channel_id=1, source_target_pairs={{0,11},{1,12},{2,13},{3,14},{4,15},{5,0},{6,1},{7,2},{8,3},{9,4},{... | collective-permute-start | bytes 196616 | tf_op jit(solution)/shard_map/ppermute | solution.py:27
  106.7 10.2 %copy-start.14 = (f32[1,16384]{1,0:T(1,128)}, f32[1,16384]{1,0:T(1,128)S(1)}, u32[]{:S(2)}) copy-start(f32[1,16384]{1,0:T(1,128)S(1)} %collective-permute-done.6) | copy-start | bytes 196612
  106.7 7.6 %collective-permute-start.11 = (f32[1,16384]{1,0:T(1,128)S(1)}, f32[1,16384]{1,0:T(1,128)S(1)}, u32[]{:S(2)}, u32[]{:S(2)}) collective-permute-start(f32[1,16384]{1,0:T(1,128)S(1)} %get-tuple-element.25), channel_id=1, source_target_pairs={{0,12},{1,13},{2,14},{3,15},{4,0},{5,1},{6,2},{7,3},{8,4},{9,5},{1... | collective-permute-start | bytes 196616 | tf_op jit(solution)/shard_map/ppermute | solution.py:27
  109.6 7.3 %copy-start.15 = (f32[1,16384]{1,0:T(1,128)}, f32[1,16384]{1,0:T(1,128)S(1)}, u32[]{:S(2)}) copy-start(f32[1,16384]{1,0:T(1,128)S(1)} %collective-permute-done.7) | copy-start | bytes 196612
  109.6 4.8 %collective-permute-start.12 = (f32[1,16384]{1,0:T(1,128)S(1)}, f32[1,16384]{1,0:T(1,128)S(1)}, u32[]{:S(2)}, u32[]{:S(2)}) collective-permute-start(f32[1,16384]{1,0:T(1,128)S(1)} %get-tuple-element.24), channel_id=1, source_target_pairs={{0,13},{1,14},{2,15},{3,0},{4,1},{5,2},{6,3},{7,4},{8,5},{9,6},{10... | collective-permute-start | bytes 196616 | tf_op jit(solution)/shard_map/ppermute | solution.py:27
  111.1 5.8 %copy-start.16 = (f32[1,16384]{1,0:T(1,128)}, f32[1,16384]{1,0:T(1,128)S(1)}, u32[]{:S(2)}) copy-start(f32[1,16384]{1,0:T(1,128)S(1)} %collective-permute-done.8) | copy-start | bytes 196612
  111.1 4.9 %collective-permute-start.13 = (f32[1,16384]{1,0:T(1,128)S(1)}, f32[1,16384]{1,0:T(1,128)S(1)}, u32[]{:S(2)}, u32[]{:S(2)}) collective-permute-start(f32[1,16384]{1,0:T(1,128)S(1)} %get-tuple-element.23), channel_id=1, source_target_pairs={{0,14},{1,15},{2,0},{3,1},{4,2},{5,3},{6,4},{7,5},{8,6},{9,7},{10,... | collective-permute-start | bytes 196616 | tf_op jit(solution)/shard_map/ppermute | solution.py:27
  113.6 3.3 %copy-start.17 = (f32[1,16384]{1,0:T(1,128)}, f32[1,16384]{1,0:T(1,128)S(1)}, u32[]{:S(2)}) copy-start(f32[1,16384]{1,0:T(1,128)S(1)} %collective-permute-done.9) | copy-start | bytes 196612
  113.6 3.2 %collective-permute-start.14 = (f32[1,16384]{1,0:T(1,128)S(1)}, f32[1,16384]{1,0:T(1,128)S(1)}, u32[]{:S(2)}, u32[]{:S(2)}) collective-permute-start(f32[1,16384]{1,0:T(1,128)S(1)} %get-tuple-element.22), channel_id=1, source_target_pairs={{0,15},{1,0},{2,1},{3,2},{4,3},{5,4},{6,5},{7,6},{8,7},{9,8},{10,9... | collective-permute-start | bytes 196616 | tf_op jit(solution)/shard_map/ppermute | solution.py:27
  114.3 2.5 %copy-start.18 = (f32[1,16384]{1,0:T(1,128)}, f32[1,16384]{1,0:T(1,128)S(1)}, u32[]{:S(2)}) copy-start(f32[1,16384]{1,0:T(1,128)S(1)} %collective-permute-done.10) | copy-start | bytes 196612
  114.3 2.5 %copy-start.19 = (f32[1,16384]{1,0:T(1,128)}, f32[1,16384]{1,0:T(1,128)S(1)}, u32[]{:S(2)}) copy-start(f32[1,16384]{1,0:T(1,128)S(1)} %collective-permute-done.11) | copy-start | bytes 196612
  114.4 2.5 %copy-start.20 = (f32[1,16384]{1,0:T(1,128)}, f32[1,16384]{1,0:T(1,128)S(1)}, u32[]{:S(2)}) copy-start(f32[1,16384]{1,0:T(1,128)S(1)} %collective-permute-done.12) | copy-start | bytes 196612
  116.0 0.9 copy-start.21
  116.9 0.6 copy-start.22
  146.2 4.6 %copy-start.3 = (bf16[384,16,128]{0,2,1:T(8,128)(2,1)S(1)}, bf16[384,16,128]{0,2,1:T(8,128)(2,1)}, u32[]{:S(2)}) copy-start(bf16[384,16,128]{0,2,1:T(8,128)(2,1)} %copy-done.2) | copy-start | bytes 4718596
  146.2 41.6 %all-to-all-start.2 = ((bf16[16,384,128]{1,2,0:T(8,128)(2,1)}), bf16[16,384,128]{1,2,0:T(8,128)(2,1)}, u32[]{:S(2)}, u32[]{:S(2)}) async-start(bf16[16,384,128]{1,2,0:T(8,128)(2,1)} %get-tuple-element.21), calls=%async_computation.2 | async-start | bytes 3145728 | tf_op jit(solution)/shard_map/all_to_all | solution.py:91
  152.3 1.7 copy-start.7
  154.1 2.7 %copy-start.5 = (bf16[16,384,384]{2,1,0:T(8,128)(2,1)}, bf16[16,384,384]{2,1,0:T(8,128)(2,1)S(1)}, u32[]{:S(2)}) copy-start(bf16[16,384,384]{2,1,0:T(8,128)(2,1)S(1)} %select_convert_fusion) | copy-start | bytes 14155780
  168.0 6.3 %copy-start.10 = (bf16[384,2048]{1,0:T(8,128)(2,1)S(1)}, bf16[384,2048]{1,0:T(8,128)(2,1)}, u32[]{:S(2)}) copy-start(bf16[384,2048]{1,0:T(8,128)(2,1)} %param.5) | copy-start | bytes 4718596
  174.4 4.1 %copy-start.12 = (bf16[2,8,128,128]{3,2,1,0:T(8,128)(2,1)}, bf16[2,8,128,128]{3,2,1,0:T(8,128)(2,1)S(1)}, u32[]{:S(2)}) copy-start(bf16[2,8,128,128]{3,2,1,0:T(8,128)(2,1)S(1)} %copy.110) | copy-start | bytes 1572868
  178.4 2.6 %copy-start.13 = (bf16[2,8,128,128]{3,2,1,0:T(8,128)(2,1)S(1)}, bf16[2,8,128,128]{3,2,1,0:T(8,128)(2,1)}, u32[]{:S(2)}) copy-start(bf16[2,8,128,128]{3,2,1,0:T(8,128)(2,1)} %copy-done.12) | copy-start | bytes 1572868
  181.1 1.4 copy-start.9
